TPU v7x, 256 devices: a whole 4x4x8 slice. The times are simulated.
256 devices in a mesh: ta: 4 (over x_lo, core), gz: 4 (over y), gy: 16 (over z, x_hi).
Axes of the slice: x: 4 (x_hi: 2, x_lo: 2; x = x_hi * 2 + x_lo), y: 4, z: 8, core: 2. Of those that a mesh axis runs over, the one named last changes fastest.
Arguments:
- eigenvectors: bfloat16 [2, 3, 96, 294912], P(None, None, None, ('ta', 'gz', 'gy')), parts along dimension 3, may hold values from -0.015625 to 0.015625
- gauge_links: bfloat16 [2, 3, 3, 3, 294912], P(None, None, None, None, ('ta', 'gz', 'gy')), parts along dimension 4, may hold values from -1.796875 to 1.796875
- solutions: bfloat16 [2, 3, 4, 96, 294912], P(None, None, None, None, ('ta', 'gz', 'gy')), parts along dimension 4, may hold values from -6 to 6
- momenta: int32 [4, 3], replicated, may hold values from -2 to 2
- solution_order: int32 [96], replicated, may hold values from 0 to 95, each once
Outputs:
- meson: float32 [1536, 4, 2, 384], P(('ta', 'gz', 'gy')), parts along dimension 0
There are 4 independent parts, one for each index of `ta`. A program takes and returns all parts, laid end to end along the dimension named above; an argument that names none is the same for every part. Nothing has to cross between parts.
Inputs may be any that keep to these rules, and one draw needn't show every extreme that they name: `solution_order`: each solution appears once.
All inputs are finite; a program needn't handle non-finite values.
Results may differ from a plain program's by a relative error of at most 0.0034.
Values may be sent and summed in bfloat16 or wider, within the bound.
No kernel may reach another device: no remote copies, remote signals or barrier semaphores. Data moves between devices by JAX's collectives and lax.ppermute only.
A program may use at most 192 MiB of HBM per device.

v0:
```python
import functools

import jax
import jax.numpy as jnp
from jax import lax
from jax.experimental import pallas as pl
from jax.experimental.pallas import tpu as pltpu
from jax.sharding import PartitionSpec as P

NEV = 96
COLS = 384
X = 48
LZ = 48
NY = 48
YD = 3
ZD = 8
PLANE = YD * X
SITES = ZD * PLANE
TILE = 128
TILES = SITES // TILE
NMOM = 4
NZ_DEVICES = 4
EDGE_Y = ZD * X
EDGE_Z = 256
ROWS = 6 * NEV
LINK_ROWS = 32
TWO_PI = 6.283185307179586
F32 = jnp.float32
BF16 = jnp.bfloat16
VMEM = pl.BlockSpec(memory_space=pltpu.VMEM)
SMEM = pl.BlockSpec(memory_space=pltpu.SMEM)
HBM = pl.BlockSpec(memory_space=pltpu.HBM)
PARAMS = pltpu.CompilerParams(vmem_limit_bytes=30 * 1024 * 1024)


def dot(a, b, dims):
    return lax.dot_general(a, b, (dims, ((), ())), preferred_element_type=F32)


def row_site(column, row):
    return column + (column // X) * (PLANE - X) + row * X


def selector(row):
    sites = lax.broadcasted_iota(jnp.int32, (SITES, EDGE_Y), 0)
    column = lax.broadcasted_iota(jnp.int32, (1, EDGE_Y), 1)
    return (sites == row_site(column, row)).astype(F32).astype(BF16)


def periodic(product, size):
    wrapped = product - size * jnp.floor(product / size)
    return jnp.where(wrapped >= size, wrapped - size, wrapped)


def wave(turns):
    quarter = jnp.floor(turns * 4.0 + 0.5)
    angle = (turns - quarter * 0.25) * F32(TWO_PI)
    square = angle * angle
    cosine = 1.0 + square * (-0.5 + square * (1 / 24 + square * (-1 / 720 + square * (1 / 40320))))
    sine = angle * (1.0 + square * (-1 / 6 + square * (1 / 120 + square * (-1 / 5040 + square * (1 / 362880)))))
    quadrant = quarter.astype(jnp.int32) & 3
    odd = (quadrant & 1) == 1
    sign_cosine = jnp.where((quadrant == 1) | (quadrant == 2), -1.0, 1.0)
    sign_sine = jnp.where(quadrant >= 2, -1.0, 1.0)
    return jnp.where(odd, sine, cosine) * sign_cosine, jnp.where(odd, cosine, sine) * sign_sine


def prepare_kernel(
    place, momenta_hbm, vec_hbm, link_hbm, sol_hbm,
    y_up, y_down, phase, flat_link, vec, edges, sol,
    momenta, link, sems,
):
    fetches = [
        pltpu.make_async_copy(link_hbm, link, sems.at[0]),
        pltpu.make_async_copy(momenta_hbm, momenta, sems.at[1]),
        pltpu.make_async_copy(vec_hbm, vec, sems.at[2]),
        pltpu.make_async_copy(sol_hbm, sol, sems.at[3]),
    ]
    for fetch in fetches:
        fetch.start()
    edges[:, :EDGE_Y] = selector(0)
    edges[:, EDGE_Y:] = selector(YD - 1)
    fetches[0].wait()
    for q in range(27):
        flat_link[2 * q : 2 * q + 2, :] = link[q // 9, (q // 3) % 3, q % 3].astype(F32)
    pad = jnp.zeros((LINK_ROWS - 18, SITES), F32)
    y_link = jnp.concatenate((flat_link[18:36, :], pad), axis=0).astype(BF16)
    fetches[1].wait()
    sites = lax.broadcasted_iota(jnp.int32, (8, SITES), 1)
    row = lax.broadcasted_iota(jnp.int32, (8, SITES), 0)
    slab = sites // PLANE
    within = sites - slab * PLANE
    line = within // X
    column = (within - line * X).astype(F32)
    slab = (slab + place[0] * ZD).astype(F32)
    line = (line + place[1] * YD).astype(F32)
    along = [jnp.zeros((8, SITES), F32) for _ in range(3)]
    for p in range(NMOM):
        for axis in range(3):
            value = momenta[(place[0] + p) & 3, axis].astype(F32)
            along[axis] = jnp.where((row & 3) == p, value, along[axis])
    x_part = periodic(along[0] * column, float(X)) / X
    y_part = periodic(along[1] * line, float(NY)) / NY
    z_part = periodic(along[2] * slab, float(LZ)) / LZ
    cosine, sine = wave(x_part + y_part + z_part)
    table = jnp.where(row < 4, cosine, sine)
    for k in range(8):
        phase[k] = jnp.broadcast_to(table[k : k + 1, :], (8, SITES))
    fetches[2].wait()
    flat = jnp.concatenate((vec[...].reshape(ROWS, SITES), y_link), axis=0)
    compact = dot(flat, edges[...], ((1,), (0,))).astype(BF16)
    y_up[...] = compact[:ROWS, :EDGE_Y]
    y_down[...] = compact[:, EDGE_Y:]
    fetches[3].wait()


def choose(mask, yes, no):
    parts = (yes.shape[0] // 8, 8, SITES)
    return jnp.where(mask[None], yes.reshape(parts), no.reshape(parts)).reshape(yes.shape)


def shift_x(block, step):
    x = lax.broadcasted_iota(jnp.int32, (8, SITES), 1) % X
    near = pltpu.roll(block, (-step) % SITES, 1)
    far = pltpu.roll(block, (step * (X - 1)) % SITES, 1)
    return choose(x == (X - 1 if step > 0 else 0), far, near)


def shift_y(near, far, step):
    line = (lax.broadcasted_iota(jnp.int32, (8, SITES), 1) // X) % YD
    return choose(line == (YD - 1 if step > 0 else 0), far, near)


def near_kernel(vec, ahead, behind):
    for block in range(6):
        here = vec[block].astype(F32)
        ahead[block] = pltpu.roll(here, SITES - X, 1).astype(BF16)
        behind[block] = pltpu.roll(here, X, 1).astype(BF16)


def shift_z(block, halo, step):
    wide = SITES + EDGE_Z
    if step > 0:
        joined = jnp.concatenate((block, halo), axis=1)
        return pltpu.roll(joined, wide - PLANE, 1)[:, :SITES]
    joined = jnp.concatenate((halo, block), axis=1)
    return pltpu.roll(joined, wide - (EDGE_Z - PLANE), 1)[:, :SITES]


def weigh(field, cosine, sine):
    real, imag = field
    return cosine * real - sine * imag, cosine * imag + sine * real


def rounded(block):
    return block.reshape(16, TILE).astype(BF16).astype(F32).reshape(2, 8, TILE)


def field_tile(direction, vec, ahead, behind, wide, rows, lanes):
    def tile(ref, block):
        return ref[block, rows, lanes].astype(F32).reshape(2, 8, TILE)

    if direction is None:
        return [(tile(vec, c), tile(vec, 3 + c)) for c in range(3)]
    forward = [(tile(ahead, c), tile(ahead, 3 + c)) for c in range(3)]
    back = [(tile(behind, c), tile(behind, 3 + c)) for c in range(3)]
    fields = []
    for a in range(3):
        real = imag = low_real = low_imag = None
        for b in range(3):
            ahead_at, behind_at = 2 * (a * 3 + b), 18 + 2 * (b * 3 + a)
            ur, ui = wide[ahead_at, :, lanes], wide[ahead_at + 1, :, lanes]
            dr, di = wide[behind_at, :, lanes], wide[behind_at + 1, :, lanes]
            vr, vi = forward[b]
            br, bi = back[b]
            terms = (ur * vr - ui * vi, ur * vi + ui * vr, dr * br + di * bi, dr * bi - di * br)
            if b == 0:
                real, imag, low_real, low_imag = terms
            else:
                real, imag, low_real, low_imag = (
                    real + terms[0], imag + terms[1], low_real + terms[2], low_imag + terms[3])
        fields.append((real - rounded(low_real), imag - rounded(low_imag)))
    return fields


def shift_all(direction, place, vec, link, halo, ahead, behind, wide):
    links = link[18 * direction : 18 * direction + 18, :]
    links = jnp.concatenate((links, jnp.zeros((14, SITES), F32)), axis=0)
    if direction == 1:
        above = jnp.concatenate((halo[0][...], jnp.zeros((LINK_ROWS, EDGE_Y), BF16)), axis=0)
        far = dot(jnp.concatenate((halo[1][...], above), axis=1), halo[2][...], ((1,), (1,)))
        ahead[...] = far[:ROWS, :].astype(BF16).reshape(6, NEV, SITES)
    if direction == 2:
        keep_up = (place[0] < NZ_DEVICES - 1).astype(F32)
        keep_down = (place[0] > 0).astype(F32)
    for block in range(6):
        here = vec[block].astype(F32)
        rows = pl.ds(block * NEV, NEV)
        if direction == 0:
            front, rear = shift_x(here, 1), shift_x(here, -1)
        elif direction == 1:
            from_devices = ahead[block].astype(F32)
            front = shift_y(halo[3][block].astype(F32), from_devices, 1)
            rear = shift_y(halo[4][block].astype(F32), from_devices, -1)
        else:
            rows = slice(2 * NEV + block % 2 * NEV, 3 * NEV + block % 2 * NEV)
            columns = slice(block // 2 * EDGE_Z, block // 2 * EDGE_Z + EDGE_Z)
            front = shift_z(here, halo[0][rows, columns].astype(F32) * keep_up, 1)
            rear = shift_z(here, halo[1][rows, columns].astype(F32) * keep_down, -1)
        ahead[block] = front.astype(BF16)
        behind[block] = rear.astype(BF16)
    if direction == 0:
        links_below = shift_x(links, -1)
    elif direction == 1:
        links_below = shift_y(pltpu.roll(links, X, 1), far[ROWS:, :], -1)
    else:
        links_below = shift_z(links, halo[1][4 * NEV :, :EDGE_Z].astype(F32) * keep_down, -1)
    for k in range(18):
        wide[k] = jnp.broadcast_to(links[k : k + 1, :], (8, SITES))
        wide[18 + k] = jnp.broadcast_to(links_below[k : k + 1, :], (8, SITES))


def field_kernel(directions, *refs):
    refs = list(refs)
    place, vec, sol, phase, link = [refs.pop(0) for _ in range(5)]
    halos = [[refs.pop(0) for _ in range(HALOS[d])] for d in directions]
    outs = [refs.pop(0) for _ in range(NMOM)]
    height = NEV * len(directions)
    leads = directions[0] is None
    if leads:
        negated = refs.pop(0)
    else:
        negated = halos[-1].pop()
    if 1 in directions:
        outs[2][NEV:, :] = halos[0].pop()[...]
    weighted = [refs.pop(0), refs.pop(0)]
    total = refs.pop(0)
    shifted = [[refs.pop(0) for _ in range(0 if d is None else 3)] for d in directions]
    for d, halo, kept in zip(directions, halos, shifted):
        if d is not None:
            shift_all(d, place, vec, link, halo, *kept)

    def fill(tile, slot, part):
        lanes = pl.ds(tile * TILE if isinstance(tile, int) else pl.multiple_of(tile * TILE, TILE), TILE)
        for e in range(2 * part, 2 * part + 2):
            for f, d in enumerate(directions):
                ahead, behind, wide = shifted[f] if shifted[f] else (None, None, None)
                fields = field_tile(d, vec, ahead, behind, wide, pl.ds(e * 16, 16), lanes)
                for p in range(NMOM):
                    cosine, sine = phase[p, :, lanes], phase[4 + p, :, lanes]
                    rows = pl.ds((p * len(directions) + f) * NEV + e * 16, 16)
                    for c in range(3):
                        real, imag = weigh(fields[c], cosine, sine)
                        weighted[slot][rows, c * TILE : (c + 1) * TILE] = real.reshape(16, TILE).astype(BF16)
                        weighted[slot][rows, (3 + c) * TILE : (4 + c) * TILE] = imag.reshape(16, TILE).astype(BF16)

    def right_hand(lanes, k, first, stop):
        pieces = []
        if first < COLS:
            pieces.append(sol[k, first : min(stop, COLS), lanes])
        if stop > COLS:
            rows = slice(max(first, COLS) - COLS, stop - COLS)
            pieces.append(sol[3 + k, rows, lanes] if k < 3 else negated[k - 3, rows, lanes])
        return pieces[0] if len(pieces) == 1 else jnp.concatenate(pieces, axis=0)

    def multiply(tile, slot, part):
        lanes = pl.ds(tile * TILE if isinstance(tile, int) else pl.multiple_of(tile * TILE, TILE), TILE)
        columns = pl.ds(part * 256, 256)
        right = jnp.concatenate([right_hand(lanes, k, part * 256, part * 256 + 256) for k in range(6)], axis=1)
        product = dot(weighted[slot][...], right, ((1,), (1,)))
        total[:, columns] = total[:, columns] + product

    for part in range(3):
        fill(0, 0, part)
    if leads:
        for c in range(3):
            negated[c] = -sol[c]
        for third in range(3):
            columns = slice(third * EDGE_Z, third * EDGE_Z + EDGE_Z)
            for b in range(2):
                at = slice(height + b * NEV, height + b * NEV + NEV)
                outs[3][at, columns] = vec[2 * third + b, :, :EDGE_Z]
                outs[1][at, columns] = vec[2 * third + b, :, SITES - EDGE_Z :]
        z_link = jnp.concatenate((link[36:54, SITES - EDGE_Z :], jnp.zeros((LINK_ROWS - 18, EDGE_Z), F32)), axis=0)
        outs[1][height + 2 * NEV :, :EDGE_Z] = z_link.astype(BF16)
        outs[1][height + 2 * NEV :, EDGE_Z:] = jnp.zeros((LINK_ROWS, 2 * EDGE_Z), BF16)
    total[...] = jnp.zeros_like(total)

    def step(i, carry):
        for tile, slot in ((4 * i, 0), (4 * i + 1, 1), (4 * i + 2, 0), (4 * i + 3, 1)):
            for part in range(3):
                multiply(tile, slot, part)
                fill(tile + 1, 1 - slot, part)
        return carry

    lax.fori_loop(0, TILES // 4, step, 0)
    for part in range(3):
        multiply(TILES - 1, 0, part)
    for p in range(NMOM):
        outs[p][:height, :] = total[p * height : (p + 1) * height, :].astype(BF16)


HALOS = {None: 0, 0: 0, 1: 7, 2: 3}


def field_block(directions, place, vec, sol, phase, link, halos):
    height = NEV * len(directions)
    leads = directions[0] is None
    scratch = [
        pltpu.VMEM((NMOM * height, 6 * TILE), BF16),
        pltpu.VMEM((NMOM * height, 6 * TILE), BF16),
        pltpu.VMEM((NMOM * height, 2 * COLS), F32),
    ]
    args = [place, vec, sol, phase, link, *halos]
    specs = [SMEM] + [VMEM] * (len(args) - 1)
    for d in directions:
        if d is not None:
            scratch += [pltpu.VMEM((6, NEV, SITES), BF16)] * 2 + [pltpu.VMEM((36, 8, SITES), F32)]
    tall = [2 * NEV + LINK_ROWS, 0, 2 * NEV] if leads else [0, 2 * NEV if 1 in directions else 0, 0]
    shapes = [jax.ShapeDtypeStruct((height + extra, 2 * COLS), BF16) for extra in (0, *tall)]
    if leads:
        shapes.append(pltpu.VMEM((3, COLS, SITES), BF16))
    return pl.pallas_call(
        functools.partial(field_kernel, directions),
        out_shape=shapes,
        in_specs=specs,
        out_specs=[VMEM] * len(shapes),
        scratch_shapes=scratch,
        compiler_params=PARAMS,
        cost_estimate=pl.CostEstimate(
            flops=8 * len(directions) * 384 * 768 * 6912, bytes_accessed=6_000_000, transcendentals=0),
        name="field_block",
    )(*args)


def total_of(terms):
    summed = terms[0].astype(F32)
    for term in terms[1:]:
        summed = summed + term.astype(F32)
    return summed


def early_kernel(*refs):
    lead, y, out = refs[:3], refs[3:7], refs[7]
    for g in range(2):
        rows = slice(g * NEV, g * NEV + NEV)
        out[g] = total_of([ref[rows, :] for ref in lead] + [y[2][NEV + g * NEV : 2 * NEV + g * NEV, :]])
    out[2] = total_of([ref[:NEV, :] for ref in y])


def middle_kernel(place, early, *refs):
    outs, held = refs[4:8], refs[8]
    for g in range(4):
        summed = early[g] if g < 3 else total_of([ref[...] for ref in refs[:4]])
        for owner in range(16):
            held[owner, g * 6 : g * 6 + 6, :] = summed[owner * 6 : owner * 6 + 6, :]
    low = place[1] & 3
    for m in range(4):
        for q in range(4):
            outs[m][q] = held[q * 4 + (low ^ m)].astype(BF16)


def second_kernel(place, own, one, two, three, *outs):
    high = place[1] // 4
    for d in range(4):
        at = (high + d) & 3
        summed = own[at].astype(F32)
        for ref in (one, two, three):
            summed = summed + ref[at].astype(F32)
        outs[d][...] = summed.astype(outs[d].dtype)


def last_kernel(own, one, two, three, order, out):
    below = lax.broadcasted_iota(jnp.int32, (COLS, COLS), 0)
    moves = (below == order[...]).astype(F32).astype(BF16)
    summed = own[...]
    for ref in (one, two, three):
        summed = summed + ref[...].astype(F32)
    for r in range(2):
        rest = summed[:, r * COLS : (r + 1) * COLS]
        moved = None
        for _ in range(3):
            part = rest.astype(BF16)
            rest = rest - part.astype(F32)
            term = dot(part, moves, ((1,), (0,)))
            moved = term if moved is None else moved + term
        for g in range(4):
            out[:, g, r, :] = moved[g * 6 : g * 6 + 6, :]


def call(kernel, shapes, specs, args, name, scratch=()):
    many = isinstance(shapes, list)
    return pl.pallas_call(
        kernel,
        out_shape=shapes,
        in_specs=specs,
        out_specs=[VMEM] * len(shapes) if many else VMEM,
        scratch_shapes=list(scratch),
        compiler_params=PARAMS,
        name=name,
    )(*args)


def prepare(place, momenta, vec, gauge_links, sol):
    shape = jax.ShapeDtypeStruct
    hbm = pltpu.MemorySpace.HBM
    made = call(
        prepare_kernel,
        [
            shape((ROWS, EDGE_Y), BF16),
            shape((ROWS + LINK_ROWS, EDGE_Y), BF16),
            pltpu.VMEM((8, 8, SITES), F32),
            pltpu.VMEM((54, SITES), F32),
            pltpu.VMEM((6, NEV, SITES), BF16),
            pltpu.VMEM((SITES, 2 * EDGE_Y), BF16),
            pltpu.VMEM((6, COLS, SITES), BF16),
        ],
        [SMEM, HBM, HBM, HBM, HBM],
        (
            place,
            pltpu.with_memory_space_constraint(momenta, hbm),
            pltpu.with_memory_space_constraint(vec, hbm),
            pltpu.with_memory_space_constraint(jnp.transpose(gauge_links, (1, 2, 3, 0, 4)), hbm),
            pltpu.with_memory_space_constraint(sol, hbm),
        ),
        "prepare",
        [
            pltpu.SMEM((NMOM, 3), jnp.int32),
            pltpu.VMEM((3, 3, 3, 2, SITES), BF16),
            pltpu.SemaphoreType.DMA((4,)),
        ],
    )
    return [*made[:2], *(in_vmem(a) for a in made[2:])]


def in_vmem(array):
    return pltpu.with_memory_space_constraint(array, pltpu.VMEM)


def body(eigenvectors, gauge_links, solutions, momenta, solution_order):
    vec = eigenvectors.reshape(6, NEV, SITES)
    sol = solutions.reshape(6, COLS, SITES)
    place = jnp.stack((lax.axis_index("gz"), lax.axis_index("gy"))).astype(jnp.int32)
    order = (jnp.tile(solution_order, 4) + (jnp.arange(COLS) // NEV) * NEV).astype(jnp.int32)[None, :]
    y_up, y_down, phase, link, vec, edges, sol = prepare(place, momenta, vec, gauge_links, sol)
    size = lax.axis_size("gy")
    y_up = lax.ppermute(y_up, "gy", [(i, (i - 1) % size) for i in range(size)])
    y_down = lax.ppermute(y_down, "gy", [(i, (i + 1) % size) for i in range(size)])
    slabs = lax.axis_size("gz")

    def across(block, k):
        return lax.ppermute(block, "gz", [(i, (i + k) % slabs) for i in range(slabs)])

    first_two = field_block((None, 0), place, vec, sol, phase, link, ())
    negated = in_vmem(first_two[4])
    from_below, from_above = across(first_two[1], 1), across(first_two[3], 3)
    near = call(near_kernel, [pltpu.VMEM((6, NEV, SITES), BF16)] * 2, [VMEM], (vec,), "near")
    near = [in_vmem(block) for block in near]
    along_y = field_block(
        (1,), place, vec, sol, phase, link, (y_up, y_down, edges, *near, first_two[2], negated))
    parts = [first_two[0], from_below, from_above]
    parts += [along_y[0], across(along_y[1], 1), across(along_y[2], 2), across(along_y[3], 3)]
    early = in_vmem(call(early_kernel, pltpu.VMEM((3, NEV, 2 * COLS), F32), [VMEM] * 7, parts, "early"))
    along_z = field_block((2,), place, vec, sol, phase, link, (from_above, from_below, negated))
    parts = [along_z[0], across(along_z[1], 1), across(along_z[2], 2), across(along_z[3], 3)]
    shape = jax.ShapeDtypeStruct
    blocks = call(
        middle_kernel,
        [shape((4, 24, 2 * COLS), BF16)] * 4,
        [SMEM] + [VMEM] * 5,
        (place, early, *parts),
        "middle",
        [pltpu.VMEM((16, 24, 2 * COLS), F32)],
    )
    parts = [blocks[0]]
    for m in range(1, 4):
        parts.append(lax.ppermute(blocks[m], "gy", [(i, i ^ m) for i in range(size)]))
    blocks = call(
        second_kernel,
        [shape((24, 2 * COLS), F32)] + [shape((24, 2 * COLS), BF16)] * 3,
        [SMEM] + [VMEM] * 4,
        (place, *parts),
        "second",
    )
    parts = [blocks[0]]
    for d in range(1, 4):
        parts.append(lax.ppermute(blocks[d], "gy", [(i, (i + 4 * d) % size) for i in range(size)]))
    return call(
        last_kernel,
        shape((6, 4, 2, COLS), F32),
        [VMEM] * 5,
        (*parts, order),
        "last",
    )


def solution(mesh):
    return jax.shard_map(
        body,
        mesh=mesh,
        in_specs=(
            P(None, None, None, ("ta", "gz", "gy")),
            P(None, None, None, None, ("ta", "gz", "gy")),
            P(None, None, None, None, ("ta", "gz", "gy")),
            P(),
            P(),
        ),
        out_specs=P(("ta", "gz", "gy"), None, None, None),
        check_vma=False,
    )
```

profile of v0, /device:TPU:2, one launch (start us, length us, event | category | flops | bytes accessed | tf_op | source)
XLA Modules:
  0.0 88.1 jit_solution(13980497009746194071)
XLA Ops:
  0.1 3.6 %prepare.1 = (bf16[576,384]{1,0:T(8,128)(2,1)S(1)}, bf16[608,384]{1,0:T(8,128)(2,1)S(1)}, f32[8,8,1152]{2,1,0:T(8,128)S(1)}, f32[54,1152]{1,0:T(8,128)S(1)}, bf1...) custom-call(s32[2]{0:T(128)S(1)} %pad_add_fusion.place.refs_0_, ...), custom_call_target="tpu_custom_call" | custom-call | tf_op jit(solution)/shard_map/prepare/pallas_call | solution.py:393
  3.6 7.5 %collective-permute-start.2 = (bf16[576,384]{1,0:T(8,128)(2,1)S(1)}, bf16[576,384]{1,0:T(8,128)(2,1)S(1)}, u32[]{:S(2)}, u32[]{:S(2)}) collective-permute-start(bf16[576,384]{1,0:T(8,128)(2,1)S(1)} %get-tuple-element.42), channel_id=1, source_target_pairs={{0,15},{1,0},{2,1},{3,2},{4,3},{5,4},{6,5},{7,6},{8,7},{9,8},{10,9... | collective-permute-start | bytes 1327112 | tf_op jit(solution)/shard_map/ppermute | solution.py:447
  11.1 13.7 %field_block.3 = (bf16[192,768]{1,0:T(8,128)(2,1)S(1)}, bf16[416,768]{1,0:T(8,128)(2,1)S(1)}, bf16[192,768]{1,0:T(8,128)(2,1)S(1)}, bf16[384,768]{1,0:T(8,128)(2,1)S(1)}, bf16[3,384,1152]{2,1,0:T(8,128)(2,1)S(1)}) custom-call(s32[2]{0:T(128)S(1)} %pad_add_fusion.place.refs_0_, bf16[6,96,1152]{2,1,0:T(8,128)(2,1)S(1)} %get-tuple-element.35.refs_1_.vec, ...), custom_call_target="tpu_custom_call" | custom-call | flops 32614907904 | bytes 6000000 | tf_op jit(solution)/shard_map/field_block/pallas_call | solution.py:323
  24.8 1.7 %collective-permute-start = (bf16[416,768]{1,0:T(8,128)(2,1)S(1)}, bf16[416,768]{1,0:T(8,128)(2,1)S(1)}, u32[]{:S(2)}, u32[]{:S(2)}) collective-permute-start(bf16[416,768]{1,0:T(8,128)(2,1)S(1)} %get-tuple-element.40), channel_id=1, source_target_pairs={{0,16},{16,32},{32,48},{48,0},{1,17},{17,33},{33,49},{49,1},{2,18}... | collective-permute-start | bytes 1916936 | tf_op jit(solution)/shard_map/ppermute | solution.py:452
  26.5 1.7 %collective-permute-start.1 = (bf16[384,768]{1,0:T(8,128)(2,1)S(1)}, bf16[384,768]{1,0:T(8,128)(2,1)S(1)}, u32[]{:S(2)}, u32[]{:S(2)}) collective-permute-start(bf16[384,768]{1,0:T(8,128)(2,1)S(1)} %get-tuple-element.41), channel_id=1, source_target_pairs={{0,48},{16,0},{32,16},{48,32},{1,49},{17,1},{33,17},{49,33},{2,50}... | collective-permute-start | bytes 1769480 | tf_op jit(solution)/shard_map/ppermute | solution.py:452
  29.0 9.1 %field_block.4 = (bf16[96,768]{1,0:T(8,128)(2,1)S(1)}, bf16[96,768]{1,0:T(8,128)(2,1)S(1)}, bf16[288,768]{1,0:T(8,128)(2,1)S(1)}, bf16[96,768]{1,0:T(8,128)(2,1)S(1)}) custom-call(s32[2]{0:T(128)S(1)} %pad_add_fusion.place.refs_0_, bf16[6,96,1152]{2,1,0:T(8,128)(2,1)S(1)} %get-tuple-element.35.refs_1_.vec, ...), custom_call_target="tpu_custom_call" | custom-call | flops 16307453952 | bytes 6000000 | tf_op jit(solution)/shard_map/field_block/pallas_call | solution.py:323
  38.5 2.9 %collective-permute-start.5 = (bf16[288,768]{1,0:T(8,128)(2,1)S(1)}, bf16[288,768]{1,0:T(8,128)(2,1)S(1)}, u32[]{:S(2)}, u32[]{:S(2)}) collective-permute-start(bf16[288,768]{1,0:T(8,128)(2,1)S(1)} %get-tuple-element.51), channel_id=1, source_target_pairs={{0,32},{16,48},{32,0},{48,16},{1,33},{17,49},{33,1},{49,17},{2,34}... | collective-permute-start | bytes 1327112 | tf_op jit(solution)/shard_map/ppermute | solution.py:452
  41.4 1.3 %collective-permute-start.6 = (bf16[96,768]{1,0:T(8,128)(2,1)S(1)}, bf16[96,768]{1,0:T(8,128)(2,1)S(1)}, u32[]{:S(2)}, u32[]{:S(2)}) collective-permute-start(bf16[96,768]{1,0:T(8,128)(2,1)S(1)} %get-tuple-element.52), channel_id=1, source_target_pairs={{0,48},{16,0},{32,16},{48,32},{1,49},{17,1},{33,17},{49,33},{2,50}... | collective-permute-start | bytes 442376 | tf_op jit(solution)/shard_map/ppermute | solution.py:452
  42.8 8.6 %field_block.5 = (bf16[96,768]{1,0:T(8,128)(2,1)S(1)}, bf16[96,768]{1,0:T(8,128)(2,1)S(1)}, bf16[96,768]{1,0:T(8,128)(2,1)S(1)}, bf16[96,768]{1,0:T(8,128)(2,1)S(1)}) custom-call(s32[2]{0:T(128)S(1)} %pad_add_fusion.place.refs_0_, bf16[6,96,1152]{2,1,0:T(8,128)(2,1)S(1)} %get-tuple-element.35.refs_1_.vec, ...), custom_call_target="tpu_custom_call" | custom-call | flops 16307453952 | bytes 6000000 | tf_op jit(solution)/shard_map/field_block/pallas_call | solution.py:323
  52.4 2.9 %collective-permute-start.8 = (bf16[96,768]{1,0:T(8,128)(2,1)S(1)}, bf16[96,768]{1,0:T(8,128)(2,1)S(1)}, u32[]{:S(2)}, u32[]{:S(2)}) collective-permute-start(bf16[96,768]{1,0:T(8,128)(2,1)S(1)} %get-tuple-element.55), channel_id=1, source_target_pairs={{0,32},{16,48},{32,0},{48,16},{1,33},{17,49},{33,1},{49,17},{2,34}... | collective-permute-start | bytes 442376 | tf_op jit(solution)/shard_map/ppermute | solution.py:452
  55.3 1.3 %collective-permute-start.9 = (bf16[96,768]{1,0:T(8,128)(2,1)S(1)}, bf16[96,768]{1,0:T(8,128)(2,1)S(1)}, u32[]{:S(2)}, u32[]{:S(2)}) collective-permute-start(bf16[96,768]{1,0:T(8,128)(2,1)S(1)} %get-tuple-element.56), channel_id=1, source_target_pairs={{0,48},{16,0},{32,16},{48,32},{1,49},{17,1},{33,17},{49,33},{2,50}... | collective-permute-start | bytes 442376 | tf_op jit(solution)/shard_map/ppermute | solution.py:452
  57.5 3.0 %collective-permute-done.7.refs_1_ = bf16[96,768]{1,0:T(8,128)(2,1)S(1)} collective-permute-done((bf16[96,768]{1,0:T(8,128)(2,1)S(1)}, bf16[96,768]{1,0:T(8,128)(2,1)S(1)}, u32[]{:S(2)}, u32[]{:S(2)}) %collective-permute-start.7) | collective-permute-done | bytes 147488 | tf_op jit(solution)/shard_map/ppermute | solution.py:452
  60.4 1.7 %collective-permute-done.8.refs_2_ = bf16[96,768]{1,0:T(8,128)(2,1)S(1)} collective-permute-done((bf16[96,768]{1,0:T(8,128)(2,1)S(1)}, bf16[96,768]{1,0:T(8,128)(2,1)S(1)}, u32[]{:S(2)}, u32[]{:S(2)}) %collective-permute-start.8) | collective-permute-done | bytes 147488 | tf_op jit(solution)/shard_map/ppermute | solution.py:452
  63.0 1.7 %collective-permute-start.10 = (bf16[4,24,768]{2,1,0:T(8,128)(2,1)S(1)}, bf16[4,24,768]{2,1,0:T(8,128)(2,1)S(1)}, u32[]{:S(2)}, u32[]{:S(2)}) collective-permute-start(bf16[4,24,768]{2,1,0:T(8,128)(2,1)S(1)} %get-tuple-element.58), channel_id=1, source_target_pairs={{0,1},{1,0},{2,3},{3,2},{4,5},{5,4},{6,7},{7,6},{8,9},{9,8},{10,11... | collective-permute-start | bytes 442376 | tf_op jit(solution)/shard_map/ppermute | solution.py:477
  64.7 1.9 %collective-permute-start.11 = (bf16[4,24,768]{2,1,0:T(8,128)(2,1)S(1)}, bf16[4,24,768]{2,1,0:T(8,128)(2,1)S(1)}, u32[]{:S(2)}, u32[]{:S(2)}) collective-permute-start(bf16[4,24,768]{2,1,0:T(8,128)(2,1)S(1)} %get-tuple-element.59), channel_id=1, source_target_pairs={{0,2},{1,3},{2,0},{3,1},{4,6},{5,7},{6,4},{7,5},{8,10},{9,11},{10,... | collective-permute-start | bytes 442376 | tf_op jit(solution)/shard_map/ppermute | solution.py:477
  66.7 1.4 %collective-permute-start.12 = (bf16[4,24,768]{2,1,0:T(8,128)(2,1)S(1)}, bf16[4,24,768]{2,1,0:T(8,128)(2,1)S(1)}, u32[]{:S(2)}, u32[]{:S(2)}) collective-permute-start(bf16[4,24,768]{2,1,0:T(8,128)(2,1)S(1)} %get-tuple-element.60), channel_id=1, source_target_pairs={{0,3},{1,2},{2,1},{3,0},{4,7},{5,6},{6,5},{7,4},{8,11},{9,10},{10,... | collective-permute-start | bytes 442376 | tf_op jit(solution)/shard_map/ppermute | solution.py:477
  68.2 1.6 %collective-permute-done.10.one = bf16[4,24,768]{2,1,0:T(8,128)(2,1)S(1)} collective-permute-done((bf16[4,24,768]{2,1,0:T(8,128)(2,1)S(1)}, bf16[4,24,768]{2,1,0:T(8,128)(2,1)S(1)}, u32[]{:S(2)}, u32[]{:S(2)}) %collective-permute-start.10) | collective-permute-done | bytes 147488 | tf_op jit(solution)/shard_map/ppermute | solution.py:477
  69.7 1.1 %collective-permute-done.11.two = bf16[4,24,768]{2,1,0:T(8,128)(2,1)S(1)} collective-permute-done((bf16[4,24,768]{2,1,0:T(8,128)(2,1)S(1)}, bf16[4,24,768]{2,1,0:T(8,128)(2,1)S(1)}, u32[]{:S(2)}, u32[]{:S(2)}) %collective-permute-start.11) | collective-permute-done | bytes 147488 | tf_op jit(solution)/shard_map/ppermute | solution.py:477
  70.8 3.6 %collective-permute-done.12.three = bf16[4,24,768]{2,1,0:T(8,128)(2,1)S(1)} collective-permute-done((bf16[4,24,768]{2,1,0:T(8,128)(2,1)S(1)}, bf16[4,24,768]{2,1,0:T(8,128)(2,1)S(1)}, u32[]{:S(2)}, u32[]{:S(2)}) %collective-permute-start.12) | collective-permute-done | bytes 147488 | tf_op jit(solution)/shard_map/ppermute | solution.py:477
  75.0 2.7 %collective-permute-start.13 = (bf16[24,768]{1,0:T(8,128)(2,1)S(1)}, bf16[24,768]{1,0:T(8,128)(2,1)S(1)}, u32[]{:S(2)}, u32[]{:S(2)}) collective-permute-start(bf16[24,768]{1,0:T(8,128)(2,1)S(1)} %get-tuple-element.62), channel_id=1, source_target_pairs={{0,4},{1,5},{2,6},{3,7},{4,8},{5,9},{6,10},{7,11},{8,12},{9,13},{1... | collective-permute-start | bytes 110600 | tf_op jit(solution)/shard_map/ppermute | solution.py:487
  77.7 4.5 %collective-permute-start.14 = (bf16[24,768]{1,0:T(8,128)(2,1)S(1)}, bf16[24,768]{1,0:T(8,128)(2,1)S(1)}, u32[]{:S(2)}, u32[]{:S(2)}) collective-permute-start(bf16[24,768]{1,0:T(8,128)(2,1)S(1)} %get-tuple-element.63), channel_id=1, source_target_pairs={{0,8},{1,9},{2,10},{3,11},{4,12},{5,13},{6,14},{7,15},{8,0},{9,1},... | collective-permute-start | bytes 110600 | tf_op jit(solution)/shard_map/ppermute | solution.py:487
  82.2 3.1 %collective-permute-start.15 = (bf16[24,768]{1,0:T(8,128)(2,1)S(1)}, bf16[24,768]{1,0:T(8,128)(2,1)S(1)}, u32[]{:S(2)}, u32[]{:S(2)}) collective-permute-start(bf16[24,768]{1,0:T(8,128)(2,1)S(1)} %get-tuple-element.64), channel_id=1, source_target_pairs={{0,12},{1,13},{2,14},{3,15},{4,0},{5,1},{6,2},{7,3},{8,4},{9,5},{1... | collective-permute-start | bytes 110600 | tf_op jit(solution)/shard_map/ppermute | solution.py:487
  85.6 1.5 %collective-permute-done.15.three = bf16[24,768]{1,0:T(8,128)(2,1)S(1)} collective-permute-done((bf16[24,768]{1,0:T(8,128)(2,1)S(1)}, bf16[24,768]{1,0:T(8,128)(2,1)S(1)}, u32[]{:S(2)}, u32[]{:S(2)}) %collective-permute-start.15) | collective-permute-done | bytes 36896 | tf_op jit(solution)/shard_map/ppermute | solution.py:487
  87.1 1.1 %last.1 = f32[6,4,2,384]{3,2,1,0:T(2,128)} custom-call(f32[24,768]{1,0:T(8,128)S(1)} %get-tuple-element.61.own, bf16[24,768]{1,0:T(8,128)(2,1)S(1)} %collective-permute-done.13.one, bf16[24,768]{1,0:T(8,128)(2,1)S(1)} %collective-permute-done.14.two, bf16[24,768]{1,0:T(8,128)(2,1)S(1)} %collective-permute-done.15.three, s32[1,384]{1,0:T(1,128)S(1)} %fusion.1.order), custom_call_target="tpu_custom_call" | custom-call | tf_op jit(solution)/shard_map/last/pallas_call | solution.py:393
  (23 shorter events, 4.9 us)
Async XLA Ops:
  3.6 25.3 %collective-permute-start.2 = (bf16[576,384]{1,0:T(8,128)(2,1)S(1)}, bf16[576,384]{1,0:T(8,128)(2,1)S(1)}, u32[]{:S(2)}, u32[]{:S(2)}) collective-permute-start(bf16[576,384]{1,0:T(8,128)(2,1)S(1)} %get-tuple-element.42), channel_id=1, source_target_pairs={{0,15},{1,0},{2,1},{3,2},{4,3},{5,4},{6,5},{7,6},{8,7},{9,8},{10,9... | collective-permute-start | bytes 1327112 | tf_op jit(solution)/shard_map/ppermute | solution.py:447
  11.1 17.9 %collective-permute-start.3 = (bf16[608,384]{1,0:T(8,128)(2,1)S(1)}, bf16[608,384]{1,0:T(8,128)(2,1)S(1)}, u32[]{:S(2)}, u32[]{:S(2)}) collective-permute-start(bf16[608,384]{1,0:T(8,128)(2,1)S(1)} %get-tuple-element.43), channel_id=1, source_target_pairs={{0,1},{1,2},{2,3},{3,4},{4,5},{5,6},{6,7},{7,8},{8,9},{9,10},{10,1... | collective-permute-start | bytes 1400840 | tf_op jit(solution)/shard_map/ppermute | solution.py:448
  24.8 18.0 %collective-permute-start = (bf16[416,768]{1,0:T(8,128)(2,1)S(1)}, bf16[416,768]{1,0:T(8,128)(2,1)S(1)}, u32[]{:S(2)}, u32[]{:S(2)}) collective-permute-start(bf16[416,768]{1,0:T(8,128)(2,1)S(1)} %get-tuple-element.40), channel_id=1, source_target_pairs={{0,16},{16,32},{32,48},{48,0},{1,17},{17,33},{33,49},{49,1},{2,18}... | collective-permute-start | bytes 1916936 | tf_op jit(solution)/shard_map/ppermute | solution.py:452
  26.5 16.3 %collective-permute-start.1 = (bf16[384,768]{1,0:T(8,128)(2,1)S(1)}, bf16[384,768]{1,0:T(8,128)(2,1)S(1)}, u32[]{:S(2)}, u32[]{:S(2)}) collective-permute-start(bf16[384,768]{1,0:T(8,128)(2,1)S(1)} %get-tuple-element.41), channel_id=1, source_target_pairs={{0,48},{16,0},{32,16},{48,32},{1,49},{17,1},{33,17},{49,33},{2,50}... | collective-permute-start | bytes 1769480 | tf_op jit(solution)/shard_map/ppermute | solution.py:452
  38.1 17.2 %collective-permute-start.4 = (bf16[96,768]{1,0:T(8,128)(2,1)S(1)}, bf16[96,768]{1,0:T(8,128)(2,1)S(1)}, u32[]{:S(2)}, u32[]{:S(2)}) collective-permute-start(bf16[96,768]{1,0:T(8,128)(2,1)S(1)} %get-tuple-element.50), channel_id=1, source_target_pairs={{0,16},{16,32},{32,48},{48,0},{1,17},{17,33},{33,49},{49,1},{2,18}... | collective-permute-start | bytes 442376 | tf_op jit(solution)/shard_map/ppermute | solution.py:452
  38.5 18.7 %collective-permute-start.5 = (bf16[288,768]{1,0:T(8,128)(2,1)S(1)}, bf16[288,768]{1,0:T(8,128)(2,1)S(1)}, u32[]{:S(2)}, u32[]{:S(2)}) collective-permute-start(bf16[288,768]{1,0:T(8,128)(2,1)S(1)} %get-tuple-element.51), channel_id=1, source_target_pairs={{0,32},{16,48},{32,0},{48,16},{1,33},{17,49},{33,1},{49,17},{2,34}... | collective-permute-start | bytes 1327112 | tf_op jit(solution)/shard_map/ppermute | solution.py:452
  41.4 15.2 %collective-permute-start.6 = (bf16[96,768]{1,0:T(8,128)(2,1)S(1)}, bf16[96,768]{1,0:T(8,128)(2,1)S(1)}, u32[]{:S(2)}, u32[]{:S(2)}) collective-permute-start(bf16[96,768]{1,0:T(8,128)(2,1)S(1)} %get-tuple-element.52), channel_id=1, source_target_pairs={{0,48},{16,0},{32,16},{48,32},{1,49},{17,1},{33,17},{49,33},{2,50}... | collective-permute-start | bytes 442376 | tf_op jit(solution)/shard_map/ppermute | solution.py:452
  51.4 9.1 %collective-permute-start.7 = (bf16[96,768]{1,0:T(8,128)(2,1)S(1)}, bf16[96,768]{1,0:T(8,128)(2,1)S(1)}, u32[]{:S(2)}, u32[]{:S(2)}) collective-permute-start(bf16[96,768]{1,0:T(8,128)(2,1)S(1)} %get-tuple-element.54), channel_id=1, source_target_pairs={{0,16},{16,32},{32,48},{48,0},{1,17},{17,33},{33,49},{49,1},{2,18}... | collective-permute-start | bytes 442376 | tf_op jit(solution)/shard_map/ppermute | solution.py:452
  52.4 9.7 %collective-permute-start.8 = (bf16[96,768]{1,0:T(8,128)(2,1)S(1)}, bf16[96,768]{1,0:T(8,128)(2,1)S(1)}, u32[]{:S(2)}, u32[]{:S(2)}) collective-permute-start(bf16[96,768]{1,0:T(8,128)(2,1)S(1)} %get-tuple-element.55), channel_id=1, source_target_pairs={{0,32},{16,48},{32,0},{48,16},{1,33},{17,49},{33,1},{49,17},{2,34}... | collective-permute-start | bytes 442376 | tf_op jit(solution)/shard_map/ppermute | solution.py:452
  55.3 6.8 %collective-permute-start.9 = (bf16[96,768]{1,0:T(8,128)(2,1)S(1)}, bf16[96,768]{1,0:T(8,128)(2,1)S(1)}, u32[]{:S(2)}, u32[]{:S(2)}) collective-permute-start(bf16[96,768]{1,0:T(8,128)(2,1)S(1)} %get-tuple-element.56), channel_id=1, source_target_pairs={{0,48},{16,0},{32,16},{48,32},{1,49},{17,1},{33,17},{49,33},{2,50}... | collective-permute-start | bytes 442376 | tf_op jit(solution)/shard_map/ppermute | solution.py:452
  57.3 10.8 %copy-start = (s32[96]{0:T(128)S(1)}, s32[96]{0:T(128)}, u32[]{:S(2)}) copy-start(s32[96]{0:T(128)} %param.9) | copy-start | bytes 1156
  63.0 6.7 %collective-permute-start.10 = (bf16[4,24,768]{2,1,0:T(8,128)(2,1)S(1)}, bf16[4,24,768]{2,1,0:T(8,128)(2,1)S(1)}, u32[]{:S(2)}, u32[]{:S(2)}) collective-permute-start(bf16[4,24,768]{2,1,0:T(8,128)(2,1)S(1)} %get-tuple-element.58), channel_id=1, source_target_pairs={{0,1},{1,0},{2,3},{3,2},{4,5},{5,4},{6,7},{7,6},{8,9},{9,8},{10,11... | collective-permute-start | bytes 442376 | tf_op jit(solution)/shard_map/ppermute | solution.py:477
  64.7 6.0 %collective-permute-start.11 = (bf16[4,24,768]{2,1,0:T(8,128)(2,1)S(1)}, bf16[4,24,768]{2,1,0:T(8,128)(2,1)S(1)}, u32[]{:S(2)}, u32[]{:S(2)}) collective-permute-start(bf16[4,24,768]{2,1,0:T(8,128)(2,1)S(1)} %get-tuple-element.59), channel_id=1, source_target_pairs={{0,2},{1,3},{2,0},{3,1},{4,6},{5,7},{6,4},{7,5},{8,10},{9,11},{10,... | collective-permute-start | bytes 442376 | tf_op jit(solution)/shard_map/ppermute | solution.py:477
  66.7 7.7 %collective-permute-start.12 = (bf16[4,24,768]{2,1,0:T(8,128)(2,1)S(1)}, bf16[4,24,768]{2,1,0:T(8,128)(2,1)S(1)}, u32[]{:S(2)}, u32[]{:S(2)}) collective-permute-start(bf16[4,24,768]{2,1,0:T(8,128)(2,1)S(1)} %get-tuple-element.60), channel_id=1, source_target_pairs={{0,3},{1,2},{2,1},{3,0},{4,7},{5,6},{6,5},{7,4},{8,11},{9,10},{10,... | collective-permute-start | bytes 442376 | tf_op jit(solution)/shard_map/ppermute | solution.py:477
  75.0 10.4 %collective-permute-start.13 = (bf16[24,768]{1,0:T(8,128)(2,1)S(1)}, bf16[24,768]{1,0:T(8,128)(2,1)S(1)}, u32[]{:S(2)}, u32[]{:S(2)}) collective-permute-start(bf16[24,768]{1,0:T(8,128)(2,1)S(1)} %get-tuple-element.62), channel_id=1, source_target_pairs={{0,4},{1,5},{2,6},{3,7},{4,8},{5,9},{6,10},{7,11},{8,12},{9,13},{1... | collective-permute-start | bytes 110600 | tf_op jit(solution)/shard_map/ppermute | solution.py:487
  77.7 7.9 %collective-permute-start.14 = (bf16[24,768]{1,0:T(8,128)(2,1)S(1)}, bf16[24,768]{1,0:T(8,128)(2,1)S(1)}, u32[]{:S(2)}, u32[]{:S(2)}) collective-permute-start(bf16[24,768]{1,0:T(8,128)(2,1)S(1)} %get-tuple-element.63), channel_id=1, source_target_pairs={{0,8},{1,9},{2,10},{3,11},{4,12},{5,13},{6,14},{7,15},{8,0},{9,1},... | collective-permute-start | bytes 110600 | tf_op jit(solution)/shard_map/ppermute | solution.py:487
  82.2 4.9 %collective-permute-start.15 = (bf16[24,768]{1,0:T(8,128)(2,1)S(1)}, bf16[24,768]{1,0:T(8,128)(2,1)S(1)}, u32[]{:S(2)}, u32[]{:S(2)}) collective-permute-start(bf16[24,768]{1,0:T(8,128)(2,1)S(1)} %get-tuple-element.64), channel_id=1, source_target_pairs={{0,12},{1,13},{2,14},{3,15},{4,0},{5,1},{6,2},{7,3},{8,4},{9,5},{1... | collective-permute-start | bytes 110600 | tf_op jit(solution)/shard_map/ppermute | solution.py:487
where the time goes:
time: 88.8 us; the launch traced here: 88.1 us
  Pallas kernels  38.5 us (43%)
  starting transfers between devices  36.2 us (41%)
  waiting for transfers between devices  13.1 us (15%)
    pallas_call x3, Pallas kernels, field_block(): pl.pallas_call(functools.partial(field_kernel, directions), out_shape=sha...  31.4 us
    ppermute x8, starting transfers between devices, across(): lax.ppermute(block, 'gz', [(i, (i + k) % slabs) for i in range(slabs)])  13.3 us
    ppermute x3, starting transfers between devices, body(): lax.ppermute(blocks[d], 'gy', [(i, (i + 4 * d) % size) for i in range(siz...  10.3 us
    ppermute x1, starting transfers between devices, body(): y_up = lax.ppermute(y_up, 'gy', [(i, (i - 1) % size) for i in range(size)])  7.49 us
    pallas_call x6, Pallas kernels, call(): pl.pallas_call(kernel, out_shape=shapes, in_specs=specs, out_specs=[VMEM]...  7.1 us
    ppermute x3, waiting for transfers between devices, body(): lax.ppermute(blocks[m], 'gy', [(i, i ^ m) for i in range(size)])  6.18 us
    ppermute x8, waiting for transfers between devices, across(): lax.ppermute(block, 'gz', [(i, (i + k) % slabs) for i in range(slabs)])  5.25 us
    ppermute x3, starting transfers between devices, body(): lax.ppermute(blocks[m], 'gy', [(i, i ^ m) for i in range(size)])  5.08 us
  transfers between devices with their start and end apart: 16, of which 8 were waited for; matrix products, arithmetic and copies ran while one was open for 0% of the time, Pallas kernels for 37%

commit v1 on v0

--- a/solution.py
+++ b/solution.py
@@ -131,11 +131,13 @@
     return choose(line == (YD - 1 if step > 0 else 0), far, near)
 
 
-def near_kernel(vec, ahead, behind):
+def near_kernel(vec, ahead, behind, above, below):
     for block in range(6):
         here = vec[block].astype(F32)
         ahead[block] = pltpu.roll(here, SITES - X, 1).astype(BF16)
         behind[block] = pltpu.roll(here, X, 1).astype(BF16)
+        above[block] = pltpu.roll(here, SITES - PLANE, 1).astype(BF16)
+        below[block] = pltpu.roll(here, PLANE, 1).astype(BF16)
 
 
 def shift_z(block, halo, step):
@@ -205,8 +207,14 @@
         else:
             rows = slice(2 * NEV + block % 2 * NEV, 3 * NEV + block % 2 * NEV)
             columns = slice(block // 2 * EDGE_Z, block // 2 * EDGE_Z + EDGE_Z)
-            front = shift_z(here, halo[0][rows, columns].astype(F32) * keep_up, 1)
-            rear = shift_z(here, halo[1][rows, columns].astype(F32) * keep_down, -1)
+            lane = lax.broadcasted_iota(jnp.int32, (NEV, EDGE_Z), 1)
+            up = pltpu.roll(halo[0][rows, columns].astype(F32) * keep_up, EDGE_Z - PLANE, 1)
+            down = pltpu.roll(halo[1][rows, columns].astype(F32) * keep_down, PLANE, 1)
+            front, rear = halo[2][block].astype(F32), halo[3][block].astype(F32)
+            top = jnp.where(lane >= EDGE_Z - PLANE, up, front[:, SITES - EDGE_Z :])
+            bottom = jnp.where(lane < PLANE, down, rear[:, :EDGE_Z])
+            front = jnp.concatenate((front[:, : SITES - EDGE_Z], top), axis=1)
+            rear = jnp.concatenate((bottom, rear[:, EDGE_Z:]), axis=1)
         ahead[block] = front.astype(BF16)
         behind[block] = rear.astype(BF16)
     if direction == 0:
@@ -300,7 +308,7 @@
         outs[p][:height, :] = total[p * height : (p + 1) * height, :].astype(BF16)
 
 
-HALOS = {None: 0, 0: 0, 1: 7, 2: 3}
+HALOS = {None: 0, 0: 0, 1: 7, 2: 5}
 
 
 def field_block(directions, place, vec, sol, phase, link, halos):
@@ -454,14 +462,14 @@
     first_two = field_block((None, 0), place, vec, sol, phase, link, ())
     negated = in_vmem(first_two[4])
     from_below, from_above = across(first_two[1], 1), across(first_two[3], 3)
-    near = call(near_kernel, [pltpu.VMEM((6, NEV, SITES), BF16)] * 2, [VMEM], (vec,), "near")
+    near = call(near_kernel, [pltpu.VMEM((6, NEV, SITES), BF16)] * 4, [VMEM], (vec,), "near")
     near = [in_vmem(block) for block in near]
     along_y = field_block(
-        (1,), place, vec, sol, phase, link, (y_up, y_down, edges, *near, first_two[2], negated))
+        (1,), place, vec, sol, phase, link, (y_up, y_down, edges, *near[:2], first_two[2], negated))
     parts = [first_two[0], from_below, from_above]
     parts += [along_y[0], across(along_y[1], 1), across(along_y[2], 2), across(along_y[3], 3)]
     early = in_vmem(call(early_kernel, pltpu.VMEM((3, NEV, 2 * COLS), F32), [VMEM] * 7, parts, "early"))
-    along_z = field_block((2,), place, vec, sol, phase, link, (from_above, from_below, negated))
+    along_z = field_block((2,), place, vec, sol, phase, link, (from_above, from_below, *near[2:], negated))
     parts = [along_z[0], across(along_z[1], 1), across(along_z[2], 2), across(along_z[3], 3)]
     shape = jax.ShapeDtypeStruct
     blocks = call(

time: 88.8 us -> 89.7 us (1.010)
  waiting for transfers between devices: 13.1 us -> 11.4 us
  starting transfers between devices: 36.2 us -> 37.9 us
    ppermute x8, starting transfers between devices: 13.3 us -> 17.6 us  [across(): lax.ppermute(block, 'gz', [(i, (i + k) % slabs) for i in range(slabs)])]
    ppermute x3, starting transfers between devices: 10.3 us -> 7.64 us  [body(): lax.ppermute(blocks[d], 'gy', [(i, (i + 4 * d) % size) for i in range(siz...]
    ppermute x1, starting transfers between devices: 0.01 us -> 2.2 us  [body(): lax.ppermute(y_down, 'gy', [(i, (i + 1) % size) for i in range(size)])]
    ppermute x1, starting transfers between devices: 7.49 us -> 5.38 us  [body(): y_up = lax.ppermute(y_up, 'gy', [(i, (i - 1) % size) for i in range(size)])]
    ppermute x3, waiting for transfers between devices: 6.18 us -> 4.6 us  [body(): lax.ppermute(blocks[m], 'gy', [(i, i ^ m) for i in range(size)])]
  transfers between devices with their start and end apart: 16 -> 16, of which waited for: 8 -> 7; matrix products, arithmetic and copies ran while one was open for 0% -> 0% of each run, Pallas kernels for 37% -> 37%
where the time goes in v1:
time: 89.7 us; the launch traced here: 88.3 us
  Pallas kernels  38.7 us (43%)
  starting transfers between devices  37.9 us (42%)
  waiting for transfers between devices  11.4 us (13%)
    pallas_call x3, Pallas kernels, field_block(): pl.pallas_call(functools.partial(field_kernel, directions), out_shape=sha...  30.9 us
    ppermute x8, starting transfers between devices, across(): lax.ppermute(block, 'gz', [(i, (i + k) % slabs) for i in range(slabs)])  17.6 us
    pallas_call x6, Pallas kernels, call(): pl.pallas_call(kernel, out_shape=shapes, in_specs=specs, out_specs=[VMEM]...  7.8 us
    ppermute x3, starting transfers between devices, body(): lax.ppermute(blocks[d], 'gy', [(i, (i + 4 * d) % size) for i in range(siz...  7.64 us
    ppermute x1, starting transfers between devices, body(): y_up = lax.ppermute(y_up, 'gy', [(i, (i - 1) % size) for i in range(size)])  5.38 us
    ppermute x3, starting transfers between devices, body(): lax.ppermute(blocks[m], 'gy', [(i, i ^ m) for i in range(size)])  5.06 us
    ppermute x8, waiting for transfers between devices, across(): lax.ppermute(block, 'gz', [(i, (i + k) % slabs) for i in range(slabs)])  4.91 us
    ppermute x3, waiting for transfers between devices, body(): lax.ppermute(blocks[m], 'gy', [(i, i ^ m) for i in range(size)])  4.6 us
  transfers between devices with their start and end apart: 16, of which 7 were waited for; matrix products, arithmetic and copies ran while one was open for 0% of the time, Pallas kernels for 37%

profile of v1, /device:TPU:2, one launch (start us, length us, event | category | flops | bytes accessed | tf_op | source)
XLA Modules:
  0.0 88.3 jit_solution(1530786699975120349)
XLA Ops:
  0.1 3.6 %prepare.1 = (bf16[576,384]{1,0:T(8,128)(2,1)S(1)}, bf16[608,384]{1,0:T(8,128)(2,1)S(1)}, f32[8,8,1152]{2,1,0:T(8,128)S(1)}, f32[54,1152]{1,0:T(8,128)S(1)}, bf1...) custom-call(s32[2]{0:T(128)S(1)} %pad_add_fusion.place.refs_0_, ...), custom_call_target="tpu_custom_call" | custom-call | tf_op jit(solution)/shard_map/prepare/pallas_call | solution.py:401
  3.6 2.2 %collective-permute-start.3 = (bf16[608,384]{1,0:T(8,128)(2,1)S(1)}, bf16[608,384]{1,0:T(8,128)(2,1)S(1)}, u32[]{:S(2)}, u32[]{:S(2)}) collective-permute-start(bf16[608,384]{1,0:T(8,128)(2,1)S(1)} %get-tuple-element.45), channel_id=1, source_target_pairs={{0,1},{1,2},{2,3},{3,4},{4,5},{5,6},{6,7},{7,8},{8,9},{9,10},{10,1... | collective-permute-start | bytes 1400840 | tf_op jit(solution)/shard_map/ppermute | solution.py:456
  5.8 5.4 %collective-permute-start.2 = (bf16[576,384]{1,0:T(8,128)(2,1)S(1)}, bf16[576,384]{1,0:T(8,128)(2,1)S(1)}, u32[]{:S(2)}, u32[]{:S(2)}) collective-permute-start(bf16[576,384]{1,0:T(8,128)(2,1)S(1)} %get-tuple-element.44), channel_id=1, source_target_pairs={{0,15},{1,0},{2,1},{3,2},{4,3},{5,4},{6,5},{7,6},{8,7},{9,8},{10,9... | collective-permute-start | bytes 1327112 | tf_op jit(solution)/shard_map/ppermute | solution.py:455
  11.2 13.7 %field_block.3 = (bf16[192,768]{1,0:T(8,128)(2,1)S(1)}, bf16[416,768]{1,0:T(8,128)(2,1)S(1)}, bf16[192,768]{1,0:T(8,128)(2,1)S(1)}, bf16[384,768]{1,0:T(8,128)(2,1)S(1)}, bf16[3,384,1152]{2,1,0:T(8,128)(2,1)S(1)}) custom-call(s32[2]{0:T(128)S(1)} %pad_add_fusion.place.refs_0_, bf16[6,96,1152]{2,1,0:T(8,128)(2,1)S(1)} %get-tuple-element.37.refs_1_.vec, ...), custom_call_target="tpu_custom_call" | custom-call | flops 32614907904 | bytes 6000000 | tf_op jit(solution)/shard_map/field_block/pallas_call | solution.py:331
  24.9 1.7 %collective-permute-start = (bf16[416,768]{1,0:T(8,128)(2,1)S(1)}, bf16[416,768]{1,0:T(8,128)(2,1)S(1)}, u32[]{:S(2)}, u32[]{:S(2)}) collective-permute-start(bf16[416,768]{1,0:T(8,128)(2,1)S(1)} %get-tuple-element.42), channel_id=1, source_target_pairs={{0,16},{16,32},{32,48},{48,0},{1,17},{17,33},{33,49},{49,1},{2,18}... | collective-permute-start | bytes 1916936 | tf_op jit(solution)/shard_map/ppermute | solution.py:460
  26.5 1.7 %collective-permute-start.1 = (bf16[384,768]{1,0:T(8,128)(2,1)S(1)}, bf16[384,768]{1,0:T(8,128)(2,1)S(1)}, u32[]{:S(2)}, u32[]{:S(2)}) collective-permute-start(bf16[384,768]{1,0:T(8,128)(2,1)S(1)} %get-tuple-element.43), channel_id=1, source_target_pairs={{0,48},{16,0},{32,16},{48,32},{1,49},{17,1},{33,17},{49,33},{2,50}... | collective-permute-start | bytes 1769480 | tf_op jit(solution)/shard_map/ppermute | solution.py:460
  28.3 1.5 %near.1 = (bf16[6,96,1152]{2,1,0:T(8,128)(2,1)S(1)}, bf16[6,96,1152]{2,1,0:T(8,128)(2,1)S(1)}, bf16[6,96,1152]{2,1,0:T(8,128)(2,1)S(1)}, bf16[6,96,1152]{2,1,0:T(8,128)(2,1)S(1)}) custom-call(bf16[6,96,1152]{2,1,0:T(8,128)(2,1)S(1)} %get-tuple-element.37.refs_1_.vec), custom_call_target="tpu_custom_call" | custom-call | tf_op jit(solution)/shard_map/near/pallas_call | solution.py:401
  29.8 9.2 %field_block.4 = (bf16[96,768]{1,0:T(8,128)(2,1)S(1)}, bf16[96,768]{1,0:T(8,128)(2,1)S(1)}, bf16[288,768]{1,0:T(8,128)(2,1)S(1)}, bf16[96,768]{1,0:T(8,128)(2,1)S(1)}) custom-call(s32[2]{0:T(128)S(1)} %pad_add_fusion.place.refs_0_, bf16[6,96,1152]{2,1,0:T(8,128)(2,1)S(1)} %get-tuple-element.37.refs_1_.vec, ...), custom_call_target="tpu_custom_call" | custom-call | flops 16307453952 | bytes 6000000 | tf_op jit(solution)/shard_map/field_block/pallas_call | solution.py:331
  39.0 2.5 %collective-permute-start.5 = (bf16[288,768]{1,0:T(8,128)(2,1)S(1)}, bf16[288,768]{1,0:T(8,128)(2,1)S(1)}, u32[]{:S(2)}, u32[]{:S(2)}) collective-permute-start(bf16[288,768]{1,0:T(8,128)(2,1)S(1)} %get-tuple-element.53), channel_id=1, source_target_pairs={{0,32},{16,48},{32,0},{48,16},{1,33},{17,49},{33,1},{49,17},{2,34}... | collective-permute-start | bytes 1327112 | tf_op jit(solution)/shard_map/ppermute | solution.py:460
  41.5 0.7 collective-permute-start.4
  42.1 2.6 %collective-permute-start.6 = (bf16[96,768]{1,0:T(8,128)(2,1)S(1)}, bf16[96,768]{1,0:T(8,128)(2,1)S(1)}, u32[]{:S(2)}, u32[]{:S(2)}) collective-permute-start(bf16[96,768]{1,0:T(8,128)(2,1)S(1)} %get-tuple-element.54), channel_id=1, source_target_pairs={{0,48},{16,0},{32,16},{48,32},{1,49},{17,1},{33,17},{49,33},{2,50}... | collective-permute-start | bytes 442376 | tf_op jit(solution)/shard_map/ppermute | solution.py:460
  44.7 8.1 %field_block.5 = (bf16[96,768]{1,0:T(8,128)(2,1)S(1)}, bf16[96,768]{1,0:T(8,128)(2,1)S(1)}, bf16[96,768]{1,0:T(8,128)(2,1)S(1)}, bf16[96,768]{1,0:T(8,128)(2,1)S(1)}) custom-call(s32[2]{0:T(128)S(1)} %pad_add_fusion.place.refs_0_, bf16[6,96,1152]{2,1,0:T(8,128)(2,1)S(1)} %get-tuple-element.37.refs_1_.vec, ...), custom_call_target="tpu_custom_call" | custom-call | flops 16307453952 | bytes 6000000 | tf_op jit(solution)/shard_map/field_block/pallas_call | solution.py:331
  52.9 8.5 %collective-permute-start.8 = (bf16[96,768]{1,0:T(8,128)(2,1)S(1)}, bf16[96,768]{1,0:T(8,128)(2,1)S(1)}, u32[]{:S(2)}, u32[]{:S(2)}) collective-permute-start(bf16[96,768]{1,0:T(8,128)(2,1)S(1)} %get-tuple-element.59), channel_id=1, source_target_pairs={{0,32},{16,48},{32,0},{48,16},{1,33},{17,49},{33,1},{49,17},{2,34}... | collective-permute-start | bytes 442376 | tf_op jit(solution)/shard_map/ppermute | solution.py:460
  61.6 1.4 %collective-permute-done.7.refs_1_ = bf16[96,768]{1,0:T(8,128)(2,1)S(1)} collective-permute-done((bf16[96,768]{1,0:T(8,128)(2,1)S(1)}, bf16[96,768]{1,0:T(8,128)(2,1)S(1)}, u32[]{:S(2)}, u32[]{:S(2)}) %collective-permute-start.7) | collective-permute-done | bytes 147488 | tf_op jit(solution)/shard_map/ppermute | solution.py:460
  63.0 3.0 %collective-permute-done.8.refs_2_ = bf16[96,768]{1,0:T(8,128)(2,1)S(1)} collective-permute-done((bf16[96,768]{1,0:T(8,128)(2,1)S(1)}, bf16[96,768]{1,0:T(8,128)(2,1)S(1)}, u32[]{:S(2)}, u32[]{:S(2)}) %collective-permute-start.8) | collective-permute-done | bytes 147488 | tf_op jit(solution)/shard_map/ppermute | solution.py:460
  66.5 0.9 middle.1
  67.5 4.9 %collective-permute-start.12 = (bf16[4,24,768]{2,1,0:T(8,128)(2,1)S(1)}, bf16[4,24,768]{2,1,0:T(8,128)(2,1)S(1)}, u32[]{:S(2)}, u32[]{:S(2)}) collective-permute-start(bf16[4,24,768]{2,1,0:T(8,128)(2,1)S(1)} %get-tuple-element.64), channel_id=1, source_target_pairs={{0,3},{1,2},{2,1},{3,0},{4,7},{5,6},{6,5},{7,4},{8,11},{9,10},{10,... | collective-permute-start | bytes 442376 | tf_op jit(solution)/shard_map/ppermute | solution.py:485
  72.5 1.6 %collective-permute-done.10.one = bf16[4,24,768]{2,1,0:T(8,128)(2,1)S(1)} collective-permute-done((bf16[4,24,768]{2,1,0:T(8,128)(2,1)S(1)}, bf16[4,24,768]{2,1,0:T(8,128)(2,1)S(1)}, u32[]{:S(2)}, u32[]{:S(2)}) %collective-permute-start.10) | collective-permute-done | bytes 147488 | tf_op jit(solution)/shard_map/ppermute | solution.py:485
  74.1 3.0 %collective-permute-done.12.three = bf16[4,24,768]{2,1,0:T(8,128)(2,1)S(1)} collective-permute-done((bf16[4,24,768]{2,1,0:T(8,128)(2,1)S(1)}, bf16[4,24,768]{2,1,0:T(8,128)(2,1)S(1)}, u32[]{:S(2)}, u32[]{:S(2)}) %collective-permute-start.12) | collective-permute-done | bytes 147488 | tf_op jit(solution)/shard_map/ppermute | solution.py:485
  77.8 4.4 %collective-permute-start.14 = (bf16[24,768]{1,0:T(8,128)(2,1)S(1)}, bf16[24,768]{1,0:T(8,128)(2,1)S(1)}, u32[]{:S(2)}, u32[]{:S(2)}) collective-permute-start(bf16[24,768]{1,0:T(8,128)(2,1)S(1)} %get-tuple-element.67), channel_id=1, source_target_pairs={{0,8},{1,9},{2,10},{3,11},{4,12},{5,13},{6,14},{7,15},{8,0},{9,1},... | collective-permute-start | bytes 110600 | tf_op jit(solution)/shard_map/ppermute | solution.py:495
  82.2 3.2 %collective-permute-start.15 = (bf16[24,768]{1,0:T(8,128)(2,1)S(1)}, bf16[24,768]{1,0:T(8,128)(2,1)S(1)}, u32[]{:S(2)}, u32[]{:S(2)}) collective-permute-start(bf16[24,768]{1,0:T(8,128)(2,1)S(1)} %get-tuple-element.68), channel_id=1, source_target_pairs={{0,12},{1,13},{2,14},{3,15},{4,0},{5,1},{6,2},{7,3},{8,4},{9,5},{1... | collective-permute-start | bytes 110600 | tf_op jit(solution)/shard_map/ppermute | solution.py:495
  85.4 0.8 collective-permute-done.14.two
  86.2 1.1 %collective-permute-done.15.three = bf16[24,768]{1,0:T(8,128)(2,1)S(1)} collective-permute-done((bf16[24,768]{1,0:T(8,128)(2,1)S(1)}, bf16[24,768]{1,0:T(8,128)(2,1)S(1)}, u32[]{:S(2)}, u32[]{:S(2)}) %collective-permute-start.15) | collective-permute-done | bytes 36896 | tf_op jit(solution)/shard_map/ppermute | solution.py:495
  87.3 1.1 %last.1 = f32[6,4,2,384]{3,2,1,0:T(2,128)} custom-call(f32[24,768]{1,0:T(8,128)S(1)} %get-tuple-element.65.own, bf16[24,768]{1,0:T(8,128)(2,1)S(1)} %collective-permute-done.13.one, bf16[24,768]{1,0:T(8,128)(2,1)S(1)} %collective-permute-done.14.two, bf16[24,768]{1,0:T(8,128)(2,1)S(1)} %collective-permute-done.15.three, s32[1,384]{1,0:T(1,128)S(1)} %fusion.1.order), custom_call_target="tpu_custom_call" | custom-call | tf_op jit(solution)/shard_map/last/pallas_call | solution.py:401
  (23 shorter events, 1.8 us)
Async XLA Ops:
  3.6 26.1 %collective-permute-start.3 = (bf16[608,384]{1,0:T(8,128)(2,1)S(1)}, bf16[608,384]{1,0:T(8,128)(2,1)S(1)}, u32[]{:S(2)}, u32[]{:S(2)}) collective-permute-start(bf16[608,384]{1,0:T(8,128)(2,1)S(1)} %get-tuple-element.45), channel_id=1, source_target_pairs={{0,1},{1,2},{2,3},{3,4},{4,5},{5,6},{6,7},{7,8},{8,9},{9,10},{10,1... | collective-permute-start | bytes 1400840 | tf_op jit(solution)/shard_map/ppermute | solution.py:456
  5.8 23.9 %collective-permute-start.2 = (bf16[576,384]{1,0:T(8,128)(2,1)S(1)}, bf16[576,384]{1,0:T(8,128)(2,1)S(1)}, u32[]{:S(2)}, u32[]{:S(2)}) collective-permute-start(bf16[576,384]{1,0:T(8,128)(2,1)S(1)} %get-tuple-element.44), channel_id=1, source_target_pairs={{0,15},{1,0},{2,1},{3,2},{4,3},{5,4},{6,5},{7,6},{8,7},{9,8},{10,9... | collective-permute-start | bytes 1327112 | tf_op jit(solution)/shard_map/ppermute | solution.py:455
  24.9 19.8 %collective-permute-start = (bf16[416,768]{1,0:T(8,128)(2,1)S(1)}, bf16[416,768]{1,0:T(8,128)(2,1)S(1)}, u32[]{:S(2)}, u32[]{:S(2)}) collective-permute-start(bf16[416,768]{1,0:T(8,128)(2,1)S(1)} %get-tuple-element.42), channel_id=1, source_target_pairs={{0,16},{16,32},{32,48},{48,0},{1,17},{17,33},{33,49},{49,1},{2,18}... | collective-permute-start | bytes 1916936 | tf_op jit(solution)/shard_map/ppermute | solution.py:460
  26.5 18.2 %collective-permute-start.1 = (bf16[384,768]{1,0:T(8,128)(2,1)S(1)}, bf16[384,768]{1,0:T(8,128)(2,1)S(1)}, u32[]{:S(2)}, u32[]{:S(2)}) collective-permute-start(bf16[384,768]{1,0:T(8,128)(2,1)S(1)} %get-tuple-element.43), channel_id=1, source_target_pairs={{0,48},{16,0},{32,16},{48,32},{1,49},{17,1},{33,17},{49,33},{2,50}... | collective-permute-start | bytes 1769480 | tf_op jit(solution)/shard_map/ppermute | solution.py:460
  39.0 22.4 %collective-permute-start.5 = (bf16[288,768]{1,0:T(8,128)(2,1)S(1)}, bf16[288,768]{1,0:T(8,128)(2,1)S(1)}, u32[]{:S(2)}, u32[]{:S(2)}) collective-permute-start(bf16[288,768]{1,0:T(8,128)(2,1)S(1)} %get-tuple-element.53), channel_id=1, source_target_pairs={{0,32},{16,48},{32,0},{48,16},{1,33},{17,49},{33,1},{49,17},{2,34}... | collective-permute-start | bytes 1327112 | tf_op jit(solution)/shard_map/ppermute | solution.py:460
  41.5 19.9 %collective-permute-start.4 = (bf16[96,768]{1,0:T(8,128)(2,1)S(1)}, bf16[96,768]{1,0:T(8,128)(2,1)S(1)}, u32[]{:S(2)}, u32[]{:S(2)}) collective-permute-start(bf16[96,768]{1,0:T(8,128)(2,1)S(1)} %get-tuple-element.52), channel_id=1, source_target_pairs={{0,16},{16,32},{32,48},{48,0},{1,17},{17,33},{33,49},{49,1},{2,18}... | collective-permute-start | bytes 442376 | tf_op jit(solution)/shard_map/ppermute | solution.py:460
  42.1 19.2 %collective-permute-start.6 = (bf16[96,768]{1,0:T(8,128)(2,1)S(1)}, bf16[96,768]{1,0:T(8,128)(2,1)S(1)}, u32[]{:S(2)}, u32[]{:S(2)}) collective-permute-start(bf16[96,768]{1,0:T(8,128)(2,1)S(1)} %get-tuple-element.54), channel_id=1, source_target_pairs={{0,48},{16,0},{32,16},{48,32},{1,49},{17,1},{33,17},{49,33},{2,50}... | collective-permute-start | bytes 442376 | tf_op jit(solution)/shard_map/ppermute | solution.py:460
  52.8 10.2 %collective-permute-start.7 = (bf16[96,768]{1,0:T(8,128)(2,1)S(1)}, bf16[96,768]{1,0:T(8,128)(2,1)S(1)}, u32[]{:S(2)}, u32[]{:S(2)}) collective-permute-start(bf16[96,768]{1,0:T(8,128)(2,1)S(1)} %get-tuple-element.58), channel_id=1, source_target_pairs={{0,16},{16,32},{32,48},{48,0},{1,17},{17,33},{33,49},{49,1},{2,18}... | collective-permute-start | bytes 442376 | tf_op jit(solution)/shard_map/ppermute | solution.py:460
  52.9 13.2 %collective-permute-start.8 = (bf16[96,768]{1,0:T(8,128)(2,1)S(1)}, bf16[96,768]{1,0:T(8,128)(2,1)S(1)}, u32[]{:S(2)}, u32[]{:S(2)}) collective-permute-start(bf16[96,768]{1,0:T(8,128)(2,1)S(1)} %get-tuple-element.59), channel_id=1, source_target_pairs={{0,32},{16,48},{32,0},{48,16},{1,33},{17,49},{33,1},{49,17},{2,34}... | collective-permute-start | bytes 442376 | tf_op jit(solution)/shard_map/ppermute | solution.py:460
  61.3 5.1 %collective-permute-start.9 = (bf16[96,768]{1,0:T(8,128)(2,1)S(1)}, bf16[96,768]{1,0:T(8,128)(2,1)S(1)}, u32[]{:S(2)}, u32[]{:S(2)}) collective-permute-start(bf16[96,768]{1,0:T(8,128)(2,1)S(1)} %get-tuple-element.60), channel_id=1, source_target_pairs={{0,48},{16,0},{32,16},{48,32},{1,49},{17,1},{33,17},{49,33},{2,50}... | collective-permute-start | bytes 442376 | tf_op jit(solution)/shard_map/ppermute | solution.py:460
  61.6 10.9 %copy-start = (s32[96]{0:T(128)S(1)}, s32[96]{0:T(128)}, u32[]{:S(2)}) copy-start(s32[96]{0:T(128)} %param.9) | copy-start | bytes 1156
  67.3 6.7 %collective-permute-start.10 = (bf16[4,24,768]{2,1,0:T(8,128)(2,1)S(1)}, bf16[4,24,768]{2,1,0:T(8,128)(2,1)S(1)}, u32[]{:S(2)}, u32[]{:S(2)}) collective-permute-start(bf16[4,24,768]{2,1,0:T(8,128)(2,1)S(1)} %get-tuple-element.62), channel_id=1, source_target_pairs={{0,1},{1,0},{2,3},{3,2},{4,5},{5,4},{6,7},{7,6},{8,9},{9,8},{10,11... | collective-permute-start | bytes 442376 | tf_op jit(solution)/shard_map/ppermute | solution.py:485
  67.4 6.6 %collective-permute-start.11 = (bf16[4,24,768]{2,1,0:T(8,128)(2,1)S(1)}, bf16[4,24,768]{2,1,0:T(8,128)(2,1)S(1)}, u32[]{:S(2)}, u32[]{:S(2)}) collective-permute-start(bf16[4,24,768]{2,1,0:T(8,128)(2,1)S(1)} %get-tuple-element.63), channel_id=1, source_target_pairs={{0,2},{1,3},{2,0},{3,1},{4,6},{5,7},{6,4},{7,5},{8,10},{9,11},{10,... | collective-permute-start | bytes 442376 | tf_op jit(solution)/shard_map/ppermute | solution.py:485
  67.5 9.6 %collective-permute-start.12 = (bf16[4,24,768]{2,1,0:T(8,128)(2,1)S(1)}, bf16[4,24,768]{2,1,0:T(8,128)(2,1)S(1)}, u32[]{:S(2)}, u32[]{:S(2)}) collective-permute-start(bf16[4,24,768]{2,1,0:T(8,128)(2,1)S(1)} %get-tuple-element.64), channel_id=1, source_target_pairs={{0,3},{1,2},{2,1},{3,0},{4,7},{5,6},{6,5},{7,4},{8,11},{9,10},{10,... | collective-permute-start | bytes 442376 | tf_op jit(solution)/shard_map/ppermute | solution.py:485
  77.7 7.7 %collective-permute-start.13 = (bf16[24,768]{1,0:T(8,128)(2,1)S(1)}, bf16[24,768]{1,0:T(8,128)(2,1)S(1)}, u32[]{:S(2)}, u32[]{:S(2)}) collective-permute-start(bf16[24,768]{1,0:T(8,128)(2,1)S(1)} %get-tuple-element.66), channel_id=1, source_target_pairs={{0,4},{1,5},{2,6},{3,7},{4,8},{5,9},{6,10},{7,11},{8,12},{9,13},{1... | collective-permute-start | bytes 110600 | tf_op jit(solution)/shard_map/ppermute | solution.py:495
  77.8 8.3 %collective-permute-start.14 = (bf16[24,768]{1,0:T(8,128)(2,1)S(1)}, bf16[24,768]{1,0:T(8,128)(2,1)S(1)}, u32[]{:S(2)}, u32[]{:S(2)}) collective-permute-start(bf16[24,768]{1,0:T(8,128)(2,1)S(1)} %get-tuple-element.67), channel_id=1, source_target_pairs={{0,8},{1,9},{2,10},{3,11},{4,12},{5,13},{6,14},{7,15},{8,0},{9,1},... | collective-permute-start | bytes 110600 | tf_op jit(solution)/shard_map/ppermute | solution.py:495
  82.2 5.0 %collective-permute-start.15 = (bf16[24,768]{1,0:T(8,128)(2,1)S(1)}, bf16[24,768]{1,0:T(8,128)(2,1)S(1)}, u32[]{:S(2)}, u32[]{:S(2)}) collective-permute-start(bf16[24,768]{1,0:T(8,128)(2,1)S(1)} %get-tuple-element.68), channel_id=1, source_target_pairs={{0,12},{1,13},{2,14},{3,15},{4,0},{5,1},{6,2},{7,3},{8,4},{9,5},{1... | collective-permute-start | bytes 110600 | tf_op jit(solution)/shard_map/ppermute | solution.py:495
